TPU v7x, 128 devices: a whole 4x4x4 slice. The times are simulated.
128 devices in a mesh: bx: 8 (over x, z_lo), by: 16 (over z_hi, y, core).
Axes of the slice: x: 4, y: 4, z: 4 (z_hi: 2, z_lo: 2; z = z_hi * 2 + z_lo), core: 2. Of those that a mesh axis runs over, the one named last changes fastest.
Arguments:
- flow_field: float32 [4, 256, 384, 256], P(None, 'bx', 'by'), may hold values from -6 to 6
- patch_corners: int32 [3, 8, 512], P(None, 'bx', 'by'), may hold values from 0 to 240, as said below
- patch_learner: int32 [8, 512, 1], P('bx', 'by'), may hold values from 0 to 15; in each aligned block of 32 rows (0 to 31, 32 to 63, ..., all dimensions but the last counted through in order) at most 4 rows name the same one
- drag_target: bfloat16 [3, 8, 512], P(None, 'bx', 'by'), may hold values from -6 to 6
- embed_weight: float32 [256, 512], replicated, may hold values from -0.375 to 0.375
- mixer_weight: float32 [512, 512], replicated, may hold values from -0.25 to 0.25
- head_weight: float32 [3, 512], replicated, may hold values from -0.25 to 0.25
Outputs:
- advanced_flow: float32 [4, 256, 384, 256], P(None, 'bx', 'by')
- slot_drag: float32 [3, 8, 1024], P(None, 'bx', 'by')
- update_embed: float32 [256, 512], replicated
- update_mixer: float32 [512, 512], replicated
- update_head: float32 [3, 512], replicated
Inputs may be any that keep to these rules, and one draw needn't show every extreme that they name: `patch_corners`: each patch lies inside its brick: the first two entries are at most 16 and 8, the third at most 240. `patch_learner`: the patches of one brick name any one learner at most 4 times, and every draw has a brick that names some learner exactly 4 times.
All inputs are finite; a program needn't handle non-finite values.
Results may differ from a plain program's by a relative error of at most 0.0053.
Values may be sent and summed in bfloat16 or wider, within the bound.
A program may use at most 128 MiB of HBM per device.

v0:
```python
import jax
import jax.numpy as jnp
from jax import lax
from jax.sharding import PartitionSpec as P

PATCH = 16
CUBE = 4
CAP = 4


KAPPA = 0.15
EPSILON = 1e-06


def shifted(block, axis, distance):
    devices = range(lax.axis_size(axis))
    route = [((i - distance) % len(devices), i) for i in devices]
    return lax.ppermute(block, axis, route)


def cut_patch(volume, start_x, start_y, start_z, extent):
    anchor = jnp.zeros((), jnp.int32)
    return lax.dynamic_slice(
        volume, (anchor, start_x, start_y, start_z), (volume.shape[0], extent, extent, extent)
    )


def patch_tokens(patch, edge):
    channels = patch.shape[0]
    across = patch.shape[1] // edge
    blocks = patch.reshape(channels, across, edge, across, edge, across, edge)
    blocks = blocks.transpose(1, 3, 5, 0, 2, 4, 6)
    return blocks.reshape(across**3 * channels * edge**3)


def patch_rows(volume, starts_x, starts_y, starts_z, extent, edge):

    def single(corner_x, corner_y, corner_z):
        return patch_tokens(cut_patch(volume, corner_x, corner_y, corner_z, extent), edge).astype(
            jnp.bfloat16
        )

    return jax.vmap(single)(starts_x, starts_y, starts_z)


def place_table(learner, peers, depth):
    choose = (learner[:, None] == jnp.arange(peers, dtype=jnp.int32)[None, :]).astype(jnp.int32)
    earlier = jnp.cumsum(choose, axis=0) - choose
    within = jnp.sum(earlier * choose, axis=1)
    target_slot = learner * depth + within
    return (jnp.arange(peers * depth, dtype=jnp.int32)[:, None] == target_slot[None, :]).astype(
        jnp.float32
    )


def gelu_slope(values):
    return jax.vjp(jax.nn.gelu, values)[1](jnp.ones_like(values))[0]


def closure_grads(rows, goals, embed_weight, mixer_weight, head_weight, early):
    count = rows.shape[0]
    features, hidden = embed_weight.shape
    per_patch = rows.shape[1] // features
    inputs = rows.reshape(count * per_patch, features)
    embed_half = embed_weight.astype(jnp.bfloat16)
    mixer_half = mixer_weight.astype(jnp.bfloat16)
    first_pre = jnp.dot(inputs, embed_half, preferred_element_type=jnp.float32)
    first_act = jax.nn.gelu(first_pre).astype(jnp.bfloat16)
    second_pre = jnp.dot(first_act, mixer_half, preferred_element_type=jnp.float32)
    pooled = jnp.mean(jax.nn.gelu(second_pre).reshape(count, per_patch, hidden), axis=1)
    predicted = jnp.dot(pooled, head_weight.T, precision=lax.Precision.HIGHEST)
    misfit = 2.0 * (predicted - goals.astype(jnp.float32))
    grad_head = jnp.dot(misfit.T, pooled, precision=lax.Precision.HIGHEST)
    pooled_back = jnp.dot(misfit, head_weight, precision=lax.Precision.HIGHEST) / per_patch
    second_back = pooled_back[:, None, :] * gelu_slope(second_pre).reshape(count, per_patch, hidden)
    second_back = second_back.reshape(count * per_patch, hidden).astype(jnp.bfloat16)
    grad_mixer = lax.dot_general(
        first_act, second_back, (((0,), (0,)), ((), ())), preferred_element_type=jnp.float32
    )
    grad_head, grad_mixer = early(grad_head, grad_mixer)
    first_back = lax.dot_general(
        second_back, mixer_half, (((1,), (1,)), ((), ())), preferred_element_type=jnp.float32
    )
    first_grad = (first_back * gelu_slope(first_pre)).astype(jnp.bfloat16)
    grad_embed = lax.dot_general(
        inputs, first_grad, (((0,), (0,)), ((), ())), preferred_element_type=jnp.float32
    )
    return (predicted, grad_embed, grad_mixer, grad_head)


def normalized(gradient):
    return gradient / jnp.sqrt(jnp.mean(gradient * gradient) + EPSILON)


def unchanged(grad_head, grad_mixer):
    return (grad_head, grad_mixer)


def diffuse_local(flow_field):
    below_x = shifted(flow_field[:, -1:].astype(jnp.bfloat16), "bx", 1).astype(jnp.float32)
    above_x = shifted(flow_field[:, :1].astype(jnp.bfloat16), "bx", -1).astype(jnp.float32)
    below_y = shifted(flow_field[:, :, -1:].astype(jnp.bfloat16), "by", 1).astype(jnp.float32)
    above_y = shifted(flow_field[:, :, :1].astype(jnp.bfloat16), "by", -1).astype(jnp.float32)
    beside_all = jnp.concatenate([below_x, flow_field[:, :-1]], axis=1) + jnp.concatenate(
        [flow_field[:, 1:], above_x], axis=1
    )
    beside_all = (
        beside_all
        + jnp.concatenate([below_y, flow_field[:, :, :-1]], axis=2)
        + jnp.concatenate([flow_field[:, :, 1:], above_y], axis=2)
    )
    vertical = jnp.pad(flow_field, ((0, 0), (0, 0), (0, 0), (1, 1)))
    beside_all = beside_all + vertical[..., 2:] + vertical[..., :-2]
    return flow_field + KAPPA * (beside_all - 6.0 * flow_field)


def per_device(
    flow_field, patch_corners, patch_learner, drag_target, embed_weight, mixer_weight, head_weight
):
    advanced_flow = diffuse_local(flow_field)
    peers = lax.axis_size("by")
    corners = patch_corners[:, 0, :]
    rows = patch_rows(flow_field, corners[0], corners[1], corners[2], PATCH, CUBE)
    goals = drag_target[:, 0, :].T
    place = place_table(patch_learner[0, :, 0], peers, CAP)
    place_half = place.astype(jnp.bfloat16)
    sent_rows = jnp.dot(place_half, rows, preferred_element_type=jnp.float32).astype(jnp.bfloat16)
    sent_goals = jnp.dot(place_half, goals, preferred_element_type=jnp.float32).astype(jnp.bfloat16)
    got_rows, got_goals = (
        lax.all_to_all(sent_rows, "by", split_axis=0, concat_axis=0, tiled=True),
        lax.all_to_all(sent_goals, "by", split_axis=0, concat_axis=0, tiled=True),
    )
    predicted, grad_embed, grad_mixer, grad_head = closure_grads(
        got_rows, got_goals, embed_weight, mixer_weight, head_weight, unchanged
    )
    grad_embed, grad_mixer, grad_head = lax.psum((grad_embed, grad_mixer, grad_head), ("bx", "by"))
    slot_drag = predicted.T[:, None, :]
    return (
        advanced_flow,
        slot_drag,
        normalized(grad_embed),
        normalized(grad_mixer),
        normalized(grad_head),
    )


def solution(mesh):
    return jax.shard_map(
        per_device,
        mesh=mesh,
        in_specs=(
            P(None, "bx", "by", None),
            P(None, "bx", "by"),
            P("bx", "by", None),
            P(None, "bx", "by"),
            P(),
            P(),
            P(),
        ),
        out_specs=(P(None, "bx", "by", None), P(None, "bx", "by"), P(), P(), P()),
        check_vma=False,
    )
```

profile of v0, /device:TPU:1, one launch (start us, length us, event | category | flops | bytes accessed | tf_op | source)
XLA Modules:
  0.0 407.3 jit_solution(10023106239383261448)
XLA Ops:
  8.0 0.8 select_reduce_fusion
  11.0 9.3 %all-to-all-start.1 = ((bf16[16,4,3]{1,2,0:T(4,128)(2,1)}), bf16[16,4,3]{1,2,0:T(4,128)(2,1)S(1)}, u32[]{:S(2)}, u32[]{:S(2)}) async-start(bf16[16,4,3]{1,2,0:T(4,128)(2,1)} %copy.23), calls=%async_computation.1 | async-start | bytes 32768 | tf_op jit(solution)/shard_map/all_to_all | solution.py:131
  21.0 2.0 convert.12
  23.1 112.9 %while.1 = (s32[]{:T(128)}, bf16[4,32,24,256]{3,2,1,0:T(8,128)(2,1)S(1)}, s32[32,4]{0,1:T(4,128)S(1)}, bf16[32,4,16,16,16]{4,3,2,1,0:T(8,128)(2,1)}, s32[]{:T(128)}) while((s32[]{:T(128)}, bf16[4,32,24,256]{3,2,1,0:T(8,128)(2,1)S(1)}, s32[32,4]{0,1:T(4,128)S(1)}, bf16[32,4,16,16,16]{4,3,2,1,0:T(8,128)(2,1)}, s32[]{:T(128)}) %tuple.36), condition=%wide.while_cond, body=%wide.while_body.sunk | while | flops 2 | bytes 297081 | solution.py:23
  23.7 2.9 bitcast_dynamic-update-slice_fusion.2
  27.2 2.9 bitcast_dynamic-update-slice_fusion.2
  30.7 2.9 bitcast_dynamic-update-slice_fusion.2
  34.2 2.9 bitcast_dynamic-update-slice_fusion.2
  37.7 2.9 bitcast_dynamic-update-slice_fusion.2
  41.3 2.9 bitcast_dynamic-update-slice_fusion.2
  44.8 2.9 bitcast_dynamic-update-slice_fusion.2
  48.3 2.9 bitcast_dynamic-update-slice_fusion.2
  51.9 3.0 bitcast_dynamic-update-slice_fusion.2
  55.4 2.9 bitcast_dynamic-update-slice_fusion.2
  58.9 2.9 bitcast_dynamic-update-slice_fusion.2
  62.5 2.9 bitcast_dynamic-update-slice_fusion.2
  66.0 2.9 bitcast_dynamic-update-slice_fusion.2
  69.5 2.9 bitcast_dynamic-update-slice_fusion.2
  73.0 2.9 bitcast_dynamic-update-slice_fusion.2
  76.6 2.9 bitcast_dynamic-update-slice_fusion.2
  80.1 2.9 bitcast_dynamic-update-slice_fusion.2
  83.6 2.9 bitcast_dynamic-update-slice_fusion.2
  87.2 2.9 bitcast_dynamic-update-slice_fusion.2
  90.7 2.9 bitcast_dynamic-update-slice_fusion.2
  94.2 2.9 bitcast_dynamic-update-slice_fusion.2
  97.7 3.0 bitcast_dynamic-update-slice_fusion.2
  101.3 2.9 bitcast_dynamic-update-slice_fusion.2
  104.8 2.9 bitcast_dynamic-update-slice_fusion.2
  108.3 2.9 bitcast_dynamic-update-slice_fusion.2
  111.9 2.9 bitcast_dynamic-update-slice_fusion.2
  115.4 2.9 bitcast_dynamic-update-slice_fusion.2
  118.9 2.9 bitcast_dynamic-update-slice_fusion.2
  122.5 2.9 bitcast_dynamic-update-slice_fusion.2
  126.0 2.9 bitcast_dynamic-update-slice_fusion.2
  129.5 2.9 bitcast_dynamic-update-slice_fusion.2
  133.0 3.0 bitcast_dynamic-update-slice_fusion.2
  136.0 11.9 %copy.21 = bf16[32,4,16,16,16]{0,4,3,2,1:T(8,128)(2,1)} copy(bf16[32,4,16,16,16]{4,3,2,1,0:T(8,128)(2,1)} %get-tuple-element.12) | data formatting | bytes 2097152 | tf_op jit(solution)/shard_map/vmap()/gather | solution.py:23
  147.9 4.5 %copy.22 = bf16[32,4,4,4,4,4,4,4]{0,7,6,5,4,3,2,1:T(4,128)(2,1)S(1)} copy(bf16[32,4,4,4,4,4,4,4]{0,7,3,6,2,5,1,4:T(4,128)(2,1)} %bitcast.46) | data formatting | bytes 2097152 | tf_op jit(solution)/shard_map/vmap()/convert_element_type | solution.py:39
  152.4 2.9 convolution_convert_fusion
  155.3 4.1 %all_to_all.12 = bf16[16,4,16384]{2,1,0:T(4,128)(2,1)} reshape(bf16[64,16384]{1,0:T(8,128)(2,1)} %convolution_convert_fusion) | data formatting | bytes 4194304 | tf_op jit(solution)/shard_map/all_to_all | solution.py:130
  159.4 7.3 %all-to-all-start = ((bf16[16,4,16384]{2,1,0:T(4,128)(2,1)}), bf16[16,4,16384]{2,1,0:T(4,128)(2,1)}, u32[]{:S(2)}, u32[]{:S(2)}) async-start(bf16[16,4,16384]{2,1,0:T(4,128)(2,1)} %all_to_all.12), calls=%async_computation | async-start | bytes 4194304 | tf_op jit(solution)/shard_map/all_to_all | solution.py:130
  166.7 2.1 fusion.55
  168.8 1.6 collective-permute-start.2
  170.4 1.5 fusion.56
  172.6 2.8 collective-permute-start.1
  175.4 3.3 fusion.53
  178.7 3.1 fusion.54
  184.1 5.5 %collective-permute-done = bf16[4,1,24,256]{3,2,1,0:T(8,128)(2,1)} collective-permute-done((bf16[4,1,24,256]{3,2,1,0:T(8,128)(2,1)}, bf16[4,1,24,256]{3,2,1,0:T(8,128)(2,1)}, u32[]{:S(2)}, u32[]{:S(2)}) %collective-permute-start) | collective-permute-done | bytes 49184 | tf_op jit(solution)/shard_map/ppermute | solution.py:18
  189.6 1.5 convert_element_type.66
  191.1 1.5 convert_element_type.67
  192.6 3.7 collective-permute-done.2
  196.5 4.6 %reshape.130 = bf16[4096,256]{1,0:T(8,128)(2,1)} reshape(bf16[16,4,16384]{2,1,0:T(4,128)(2,1)} %all-to-all-done) | data formatting | bytes 4194304 | tf_op jit(solution)/shard_map/reshape | solution.py:64
  201.2 3.0 fusion.28
  204.2 5.8 %bitcast_reduce_fusion = (f32[64,512]{1,0:T(8,128)S(1)}, f32[4096,512]{1,0:T(8,128)S(1)}) fusion(f32[512,512]{1,0:T(8,128)S(1)} %copy-done.5, f32[4096,512]{1,0:T(8,128)S(1)} %fusion.28), kind=kOutput, calls=%fused_computation.23 | convolution fusion | flops 2185461760 | bytes 17956864 | tf_op jit(solution)/shard_map/dot_general | solution.py:69
  210.6 6.7 %fusion.15 = bf16[4096,512]{1,0:T(8,128)(2,1)} fusion(f32[4096,512]{1,0:T(8,128)S(1)} %get-tuple-element.60, f32[64,512]{1,0:T(8,128)S(1)} %convolution_multiply_fusion), kind=kLoop, calls=%fused_computation.22 | loop fusion | flops 39845888 | bytes 12713984 | tf_op jit(solution)/shard_map/convert_element_type | solution.py:76
  217.4 13.8 %fusion.23 = f32[256,512]{1,0:T(8,128)} fusion(bf16[4096,256]{1,0:T(8,128)(2,1)} %reshape.130, f32[4096,512]{1,0:T(8,128)} %copy-done.2, bf16[4096,512]{1,0:T(8,128)(2,1)} %fusion.15, f32[512,512]{1,0:T(8,128)} %param.12), kind=kOutput, calls=%fused_computation.36 | convolution fusion | flops 3261333504 | bytes 16252928 | tf_op jit(solution)/shard_map/dot_general | solution.py:85
  231.1 8.7 %fusion.50 = f32[512,512]{1,0:T(8,128)} fusion(bf16[4096,512]{1,0:T(8,128)(2,1)} %fusion.15, f32[4096,512]{1,0:T(8,128)} %copy-done.2), kind=kOutput, calls=%fused_computation.80 | convolution fusion | flops 2166358016 | bytes 13631488 | tf_op jit(solution)/shard_map/dot_general | solution.py:77
  239.8 7.2 %fusion.20 = f32[4,32,24,256]{3,2,1,0:T(8,128)} fusion(f32[4,32,24,256]{3,2,1,0:T(8,128)S(1)} %copy-done.1, f32[4,31,24,256]{3,2,1,0:T(8,128)} %get-tuple-element.51, f32[4,1,24,256]{3,2,1,0:T(8,128)} %convert_element_type.66, f32[4,1,24,256]{3,2,1,0:T(8,128)} %convert_element_type.67, f32[4,31,24,256]{3,2,1,0:T(8,128)} %get-tuple-element.50, ...), kind=kLoop, calls=%fused_computation.32 | loop fusion | flops 10223616 | bytes 18874368 | tf_op jit(solution)/shard_map/add | solution.py:114
  247.2 67.6 %psum.23 = f32[3,512]{1,0:T(4,128)S(1)} all-reduce(f32[3,512]{1,0:T(4,128)S(1)} %fusion.30), channel_id=1, replica_groups=mesh['bx'=8,'by'=16] {'bx','by'}, use_global_device_ids=true, to_apply=%region_7.8 | all-reduce | flops 1536 | bytes 12288 | tf_op jit(solution)/shard_map/psum | solution.py:136
  317.3 73.7 %all-reduce.4.cloned.1.call-done = (f32[256,512]{1,0:T(8,128)}, f32[512,512]{1,0:T(8,128)}) async-done(((f32[256,512]{1,0:T(8,128)}, f32[512,512]{1,0:T(8,128)}), (f32[256,512]{1,0:T(8,128)}, f32[512,512]{1,0:T(8,128)})) %all-reduce.4.cloned.1.call-update) | async-done | bytes 1572880 | tf_op jit(solution)/shard_map/psum | solution.py:136
  391.0 2.1 multiply_reduce_fusion
  393.8 2.3 broadcast_divide_fusion
  396.1 1.8 multiply_reduce_fusion.1
  398.6 1.9 broadcast_divide_fusion.1
  (105 shorter events, 28.7 us)
Async XLA Ops:
  7.2 202.9 %copy-start = (f32[3,512]{1,0:T(4,128)S(1)}, f32[3,512]{1,0:T(4,128)}, u32[]{:S(2)}) copy-start(f32[3,512]{1,0:T(4,128)} %param.13) | copy-start | bytes 18436
  11.0 148.4 %all-to-all-start.1 = ((bf16[16,4,3]{1,2,0:T(4,128)(2,1)}), bf16[16,4,3]{1,2,0:T(4,128)(2,1)S(1)}, u32[]{:S(2)}, u32[]{:S(2)}) async-start(bf16[16,4,3]{1,2,0:T(4,128)(2,1)} %copy.23), calls=%async_computation.1 | async-start | bytes 32768 | tf_op jit(solution)/shard_map/all_to_all | solution.py:131
  136.0 11.9 %copy-start.3 = (bf16[4,32,24,256]{3,2,1,0:T(8,128)(2,1)}, bf16[4,32,24,256]{3,2,1,0:T(8,128)(2,1)S(1)}, u32[]{:S(2)}) copy-start(bf16[4,32,24,256]{3,2,1,0:T(8,128)(2,1)S(1)} %get-tuple-element.113) | copy-start | bytes 4718596
  152.4 23.0 %copy-start.1 = (f32[4,32,24,256]{3,2,1,0:T(8,128)S(1)}, f32[4,32,24,256]{3,2,1,0:T(8,128)}, u32[]{:S(2)}) copy-start(f32[4,32,24,256]{3,2,1,0:T(8,128)} %param.7) | copy-start | bytes 9437188
  159.4 7.3 %copy-start.4 = (bf16[16,4,3]{1,2,0:T(4,128)(2,1)}, bf16[16,4,3]{1,2,0:T(4,128)(2,1)S(1)}, u32[]{:S(2)}) copy-start(bf16[16,4,3]{1,2,0:T(4,128)(2,1)S(1)} %all-to-all-done.1) | copy-start | bytes 1156
  159.4 37.2 %all-to-all-start = ((bf16[16,4,16384]{2,1,0:T(4,128)(2,1)}), bf16[16,4,16384]{2,1,0:T(4,128)(2,1)}, u32[]{:S(2)}, u32[]{:S(2)}) async-start(bf16[16,4,16384]{2,1,0:T(4,128)(2,1)} %all_to_all.12), calls=%async_computation | async-start | bytes 4194304 | tf_op jit(solution)/shard_map/all_to_all | solution.py:130
  166.6 224.4 %all-reduce.4.cloned.1.call-start = ((), (), s32[]{:S(2)}) async-start(), calls=%async_computation.2 | async-start | bytes 3145728 | tf_op jit(solution)/shard_map/psum | solution.py:136
  168.8 27.5 %collective-permute-start.2 = (bf16[4,32,1,256]{3,2,1,0:T(2,128)(2,1)S(1)}, bf16[4,32,1,256]{3,2,1,0:T(2,128)(2,1)S(1)}, u32[]{:S(2)}, u32[]{:S(2)}) collective-permute-start(bf16[4,32,1,256]{3,2,1,0:T(2,128)(2,1)S(1)} %get-tuple-element.53), channel_id=1, source_target_pairs={{15,0},{0,1},{1,2},{2,3},{3,4},{4,5},{5,6},{6,7},{7,8},{8,9},{9,10... | collective-permute-start | bytes 196616 | tf_op jit(solution)/shard_map/ppermute | solution.py:18
  170.4 26.0 %collective-permute-start.3 = (bf16[4,32,1,256]{3,2,1,0:T(2,128)(2,1)}, bf16[4,32,1,256]{3,2,1,0:T(2,128)(2,1)S(1)}, u32[]{:S(2)}, u32[]{:S(2)}) collective-permute-start(bf16[4,32,1,256]{3,2,1,0:T(2,128)(2,1)} %get-tuple-element.52), channel_id=1, source_target_pairs={{1,0},{2,1},{3,2},{4,3},{5,4},{6,5},{7,6},{8,7},{9,8},{10,9},{11,1... | collective-permute-start | bytes 196616 | tf_op jit(solution)/shard_map/ppermute | solution.py:18
  171.9 17.8 %collective-permute-start = (bf16[4,1,24,256]{3,2,1,0:T(8,128)(2,1)}, bf16[4,1,24,256]{3,2,1,0:T(8,128)(2,1)}, u32[]{:S(2)}, u32[]{:S(2)}) collective-permute-start(bf16[4,1,24,256]{3,2,1,0:T(8,128)(2,1)} %get-tuple-element.55), channel_id=1, source_target_pairs={{112,0},{0,16},{16,32},{32,48},{48,64},{64,80},{80,96},{96,112},{1... | collective-permute-start | bytes 147464 | tf_op jit(solution)/shard_map/ppermute | solution.py:18
  172.6 18.5 %collective-permute-start.1 = (bf16[4,1,24,256]{3,2,1,0:T(8,128)(2,1)}, bf16[4,1,24,256]{3,2,1,0:T(8,128)(2,1)}, u32[]{:S(2)}, u32[]{:S(2)}) collective-permute-start(bf16[4,1,24,256]{3,2,1,0:T(8,128)(2,1)} %get-tuple-element.54), channel_id=1, source_target_pairs={{16,0},{32,16},{48,32},{64,48},{80,64},{96,80},{112,96},{0,112},{1... | collective-permute-start | bytes 147464 | tf_op jit(solution)/shard_map/ppermute | solution.py:18
  201.2 3.0 copy-start.5
  204.2 5.9 %copy-start.2 = (f32[4096,512]{1,0:T(8,128)}, f32[4096,512]{1,0:T(8,128)S(1)}, u32[]{:S(2)}) copy-start(f32[4096,512]{1,0:T(8,128)S(1)} %fusion.28) | copy-start | bytes 25165828
Sparse Core Ops, SparseCore 0:
  239.9 151.0 all-reduce.3
where the time goes:
time: 410 us; the launch traced here: 407 us
  local copies, waits for them, and re-layouts  151 us (37%)
  waiting for transfers between devices  82.9 us (20%)
  blocking collectives  67.6 us (16%)
  matrix products  35.7 us (9%)
  other arithmetic  31.4 us (8%)
  starting transfers between devices  21.8 us (5%)
  between operations  16.3 us (4%)
    gather x96, local copies, waits for them, and re-layouts  113 us
    psum x1, waiting for transfers between devices, per_device(): lax.psum((grad_embed, grad_mixer, grad_head), ('bx', 'by'))  73.7 us
    psum x1, blocking collectives, per_device(): lax.psum((grad_embed, grad_mixer, grad_head), ('bx', 'by'))  67.6 us
    dot_general x1, matrix products, closure_grads(): lax.dot_general(inputs, first_grad, (((0,), (0,)), ((), ())), preferred_e...  13.8 us
    gather x1, local copies, waits for them, and re-layouts, cut_patch(): lax.dynamic_slice(volume, (anchor, start_x, start_y, start_z), (volume.sh...  11.9 us
    all_to_all x1, starting transfers between devices, per_device(): lax.all_to_all(sent_goals, 'by', split_axis=0, concat_axis=0, tiled=True)  9.3 us
    ppermute x4, waiting for transfers between devices, shifted(): return lax.ppermute(block, axis, route)  9.19 us
    dot_general x1, matrix products, closure_grads(): lax.dot_general(first_act, second_back, (((0,), (0,)), ((), ())), preferr...  8.69 us
  transfers between devices with their start and end apart: 7, of which 3 were waited for; matrix products, arithmetic and copies ran while one was open for 39% of the time, Pallas kernels for 0%

commit v1 on v0

v1 whole, which is shorter than its diff:
```python
import functools
import jax
import jax.numpy as jnp
from jax import lax
from jax.experimental import pallas as pl
from jax.experimental.pallas import tpu as pltpu
from jax.sharding import PartitionSpec as P

CHAN, CX, CY, CZ = 4, 32, 24, 256
PB, CAP, HID, FEAT = 32, 4, 512, 256
COLS = CHAN * CX * CY
SLAB = (CX + 2) * CY
BX, BY = 8, 16
MESH = pl.DeviceIdType.MESH
TILES = 8
KAPPA = 0.15
EPSILON = 1e-06
GELU_S = 0.7978845608028654
GELU_C = 0.044715
F32, BF16 = jnp.float32, jnp.bfloat16


def iota(shape, axis):
    return lax.broadcasted_iota(jnp.int32, shape, axis)


def gelu_and_slope(x):
    x2 = x * x
    t = jnp.tanh(x * (x2 * (GELU_S * GELU_C) + GELU_S))
    h = 0.5 * t + 0.5
    value = x * h
    return value, h + value * (1.0 - h) * (x2 * (6.0 * GELU_S * GELU_C) + 2.0 * GELU_S)


def load_flow(flow_ref, field, sems):
    copies = [
        pltpu.make_async_copy(
            flow_ref.at[pl.ds(CX * CY * c, CX * CY), pl.ds(128 * h, 128)],
            field.at[h, pl.ds(SLAB * c + CY, CX * CY)],
            sems.at[h, c],
        )
        for h in range(2)
        for c in range(CHAN)
    ]
    for copy in copies:
        copy.start()
    return copies


def level_of(field, h, y):
    return jnp.concatenate(
        [field[h, pl.ds(SLAB * c + CY + y, CX, stride=CY), :] for c in range(CHAN)], 0
    )


def upright(h, field, turned):
    for y in range(CY):
        turned[pl.ds(y * CZ + 128 * h, 128), :] = level_of(field, h, y).T


def cut(patches, corners_ref, turned, pieces):
    upper = iota((8, 128), 0) < 4
    even = iota((8, 128), 1) % 32 < 16
    for p in patches:
        x0, y0, z0 = corners_ref[0, 0, p], corners_ref[1, 0, p], corners_ref[2, 0, p]
        base = y0 * CZ + z0
        back = lax.rem(128 - x0, 128)
        for pair in range(8):
            halves = []
            for cy in (0, 2):
                both = []
                for parity in range(2):
                    fy, fz = divmod(2 * pair + parity, 4)
                    first = base + (4 * cy + fy) * CZ + fz
                    a = turned[pl.ds(first, 8, stride=4), :]
                    b = turned[pl.ds(first + 4 * CZ - 16, 8, stride=4), :]
                    both.append(
                        pltpu.roll(jnp.where(upper, a, b), back + 16 * parity, 1)
                    )
                halves.append(jnp.where(even, both[0], both[1]))
            pieces[pl.ds(16 * p, 16), pl.ds(128 * pair, 128)] = jnp.concatenate(halves, 0).astype(BF16)


def make_order(order):
    for block in range(8):
        k = iota((128, 1), 0)
        c, parity, cx, fx = k // 32, k // 16 % 2, k // 4 % 4, k % 4
        fyz = 2 * block + parity
        target = cx * FEAT + c * 64 + fx * 16 + fyz
        hit = iota((128, 4 * FEAT), 1) == target
        order[pl.ds(128 * block, 128), :] = jnp.where(hit, 1.0, 0.0).astype(BF16)


def order_rows(half, pieces, order, rows, rows_t):
    tiles = range(4 * half, 4 * half + 4)
    for cx in range(4):
        got = jnp.dot(
            pieces[pl.ds(256 * half, 256), :],
            order[:, pl.ds(FEAT * cx, FEAT)],
            preferred_element_type=F32,
        ).astype(BF16)
        for n, t in enumerate(tiles):
            rows[pl.ds(256 * t + 64 * cx, 64), :] = got[64 * n : 64 * n + 64]
    for t in tiles:
        rows_t[:, pl.ds(256 * t, 256)] = rows[pl.ds(256 * t, 256), :].T


def forward(t, rows, embed, mixer, act, act_t, slope1, slope2, pooled):
    at = pl.ds(t * 256, 256)
    for n in range(2):
        columns = pl.ds(256 * n, 256)
        pre = jnp.dot(rows[at, :], embed[:, columns], preferred_element_type=F32)
        value, slope = gelu_and_slope(pre)
        value = value.astype(BF16)
        act[at, columns] = value
        act_t[columns, at] = value.T
        slope1[at, columns] = slope
    for n in range(2):
        columns = pl.ds(256 * n, 256)
        pre = jnp.dot(act[at, :], mixer[:, columns], preferred_element_type=F32)
        value, slope = gelu_and_slope(pre)
        slope2[at, columns] = slope
        value = value.reshape(4, 4, 16, 256).sum(axis=0).sum(axis=1)
        pooled[t, :, columns] = value * (1.0 / 64)


def head_step(half, pooled_ref, goals_ref, learner_ref, head_ref, back, head_grad, slot_part):
    some = PB // 2
    first = some * half
    pooled = pooled_ref[pl.ds(4 * half, 4)].reshape(some, HID)
    head = head_ref[...]
    patch = iota((some, PB), 0) + first
    other = iota((some, PB), 1)
    learner_row = learner_ref[...]
    learner = jnp.sum(jnp.where(patch == other, learner_row, 0), axis=1, keepdims=True)
    earlier = (learner == learner_row) & (other < patch)
    within = jnp.sum(jnp.where(earlier, 1, 0), axis=1, keepdims=True)
    slot = learner * CAP + within
    place = iota((some, 128), 1) == slot
    total = jnp.zeros((some, HID), F32)
    head_rows, slot_rows = [], []
    for k in range(3):
        weight = head[k : k + 1, :]
        predicted = jnp.sum(pooled * weight, axis=1, keepdims=True)
        goal = goals_ref[k : k + 1, :].astype(F32)
        goal = jnp.sum(jnp.where(patch == other, goal, 0.0), axis=1, keepdims=True)
        misfit = 2.0 * (predicted - goal)
        total = total + misfit * weight
        head_rows.append(jnp.sum(misfit * pooled, axis=0, keepdims=True))
        slot_rows.append(jnp.sum(jnp.where(place, predicted, 0.0), axis=0, keepdims=True))
    back[pl.ds(4 * half, 4)] = (total * (1.0 / 64)).reshape(4, 4, HID)
    if half == 0:
        head_grad[...] = jnp.zeros_like(head_grad)
        slot_part[...] = jnp.zeros_like(slot_part)
    for k in range(3):
        head_grad[k : k + 1, :] += head_rows[k][:, 0:256]
        head_grad[k + 3 : k + 4, :] += head_rows[k][:, 256:512]
        slot_part[k : k + 1, :] += slot_rows[k]


def second_layer_back(t, back, slope2, second):
    at = pl.ds(t * 256, 256)
    for n in range(2):
        columns = pl.ds(256 * n, 256)
        slope = slope2[at, columns].reshape(4, 4, 16, 256)
        value = slope * back[t, :, columns][None, :, None, :]
        second[at, columns] = value.reshape(256, 256).astype(BF16)


def first_layer_back(t, second, mixer_t, slope1, first):
    at = pl.ds(t * 256, 256)
    for n in range(2):
        columns = pl.ds(256 * n, 256)
        value = jnp.dot(second[at, :], mixer_t[:, columns], preferred_element_type=F32)
        first[at, columns] = (value * slope1[at, columns]).astype(BF16)


def send_all(axis, source, target, send_sem, recv_sem):
    bx, by = lax.axis_index("bx"), lax.axis_index("by")
    me, size = (by, BY) if axis == "by" else (bx, BX)

    def step(distance, carry):
        peer = lax.rem(me + distance, size)
        pltpu.make_async_remote_copy(
            src_ref=source(peer),
            dst_ref=target,
            send_sem=send_sem,
            recv_sem=recv_sem,
            device_id=(bx, peer) if axis == "by" else (peer, by),
            device_id_type=MESH,
        ).start()
        return carry

    lax.fori_loop(1, size, step, 0)


def wait_all(buffer, sem):
    blocks = buffer.at[pl.ds(0, buffer.shape[0] - 1)]
    pltpu.make_async_copy(blocks, blocks, sem).wait()


def where_am_i():
    bx, by = lax.axis_index("bx"), lax.axis_index("by")
    div, rem = lax.div, lax.rem
    return [div(bx, 2), rem(div(by, 2), 4), div(by, 8) * 2 + rem(bx, 2), rem(by, 2)]


def device_at(place):
    x, y, z, core = place
    return (x * 2 + lax.rem(z, 2), lax.div(z, 2) * 8 + y * 2 + core)


PLANES = ((0, 1), (1, 2), (2, 0))
LINES = (2, 0, 1)


def plane_peers(job):
    place = where_am_i()
    first, second = PLANES[job]
    turns = [[lax.rem(place[axis] + d, 4) for d in range(4)] for axis in (first, second)]
    peers = []
    for d in (10, 6, 14, 9, 11, 2, 8, 5, 7, 13, 15, 1, 3, 4, 12, 0):
        for other in (0, 1) if job == 2 else (0,):
            if d == 0 and other == 0:
                continue
            there = list(place)
            there[first], there[second] = turns[0][d // 4], turns[1][d % 4]
            block = there[first] * 4 + there[second]
            if other:
                there[3] = 1 - place[3]
            if job == 2:
                block = block + 16 * there[3]
            peers.append((block, device_at(there)))
    return peers


def plane_index(job):
    place = where_am_i()
    first, second = PLANES[job]
    block = place[first] * 4 + place[second]
    return block + 16 * place[3] if job == 2 else block


def mate():
    place = where_am_i()
    place[3] = 1 - place[3]
    return device_at(place)


def partners():
    found = set()
    for y in range(4):
        for z in (0, 2):
            found.update((0, y, z, core) for core in (0, 1))
    for job in range(3):
        for d in range(16):
            there = [0, 0, 0, 0]
            there[PLANES[job][0]], there[PLANES[job][1]] = d // 4, d % 4
            for core in (0, 1) if job == 2 else (0,):
                there[3] = core
                found.add(tuple(there))
    return sorted(found - {(0, 0, 0, 0)})


def greet():
    barrier = pltpu.get_barrier_semaphore()
    here = where_am_i()
    turns = [[lax.rem(here[axis] + d, 4) for d in range(4)] for axis in range(3)]
    for x, y, z, core in partners():
        device = device_at((turns[0][x], turns[1][y], turns[2][z], 1 - here[3] if core else here[3]))
        pl.semaphore_signal(barrier, inc=1, device_id=device, device_id_type=MESH)


def send_plane(job, source, target, sems):
    for n, device in plane_peers(job):
        pltpu.make_async_remote_copy(
            src_ref=source(n),
            dst_ref=target,
            send_sem=sems[0],
            recv_sem=sems[1],
            device_id=device,
            device_id_type=MESH,
        ).start()


def send_line(axis, block, sems):
    for distance in (2, 1, 3):
        place = where_am_i()
        place[axis] = lax.rem(place[axis] + distance, 4)
        pltpu.make_async_remote_copy(
            src_ref=block,
            dst_ref=block,
            send_sem=sems[0],
            recv_sem=sems[1],
            device_id=device_at(place),
            device_id_type=MESH,
        ).start()


def send_mate(source, target, sems):
    pltpu.make_async_remote_copy(
        src_ref=source,
        dst_ref=target,
        send_sem=sems[0],
        recv_sem=sems[1],
        device_id=mate(),
        device_id_type=MESH,
    ).start()


def wait_one(buffer, sem):
    pltpu.make_async_copy(buffer, buffer, sem).wait()


def fill_faces(field, x_face, y_face):
    for h in range(2):
        for side, x in ((0, 0), (1, CX - 1)):
            layers = [field[h, pl.ds(SLAB * c + CY * (x + 1), CY), :] for c in range(CHAN)]
            x_face[side, h] = jnp.concatenate(layers, 0).astype(BF16)
        for side, y in ((0, 0), (1, CY - 1)):
            y_face[side, h] = level_of(field, h, y).astype(BF16)


def halo_copies(x_face, y_face, x_halo, y_halo, send_sems, recv_sems):
    bx, by = lax.axis_index("bx"), lax.axis_index("by")
    copies = []
    for n, (face, halo, device) in enumerate(
        (
            (x_face.at[1], x_halo.at[0], (lax.rem(bx + 1, BX), by)),
            (x_face.at[0], x_halo.at[1], (lax.rem(bx + BX - 1, BX), by)),
            (y_face.at[1], y_halo.at[0], (bx, lax.rem(by + 1, BY))),
            (y_face.at[0], y_halo.at[1], (bx, lax.rem(by + BY - 1, BY))),
        )
    ):
        copies.append(
            pltpu.make_async_remote_copy(
                src_ref=face,
                dst_ref=halo,
                send_sem=send_sems.at[n],
                recv_sem=recv_sems.at[n],
                device_id=device,
                device_id_type=MESH,
            )
        )
    return copies


def place_halos(x_halo, y_halo, field, y_edge):
    for h in range(2):
        for side, slot in ((0, 0), (1, CX + 1)):
            layers = x_halo[side, h].astype(F32)
            for c in range(CHAN):
                rows = pl.ds(SLAB * c + CY * slot, CY)
                field[h, rows, :] = layers[CY * c : CY * c + CY]
            y_edge[side, h] = y_halo[side, h].astype(F32)


def diffuse(c, field, y_edge, moved):
    row, lane = iota((CY, 128), 0), iota((CY, 128), 1)

    def column(x, carry):
        first = SLAB * c + CY + CY * x
        here = pl.ds(pl.multiple_of(first, 8), CY)
        cells = [field[h, here, :] for h in range(2)]
        down = [pltpu.roll(cells[h], 1, 1) for h in range(2)]
        up = [pltpu.roll(cells[h], 127, 1) for h in range(2)]
        below = [jnp.where(lane == 0, 0.0, down[0]), jnp.where(lane == 0, down[0], down[1])]
        above = [jnp.where(lane == 127, up[1], up[0]), jnp.where(lane == 127, 0.0, up[1])]
        for h in range(2):
            total = below[h] + above[h]
            total = total + field[h, pl.ds(pl.multiple_of(first - CY, 8), CY), :]
            total = total + field[h, pl.ds(pl.multiple_of(first + CY, 8), CY), :]
            low = y_edge[0, h, pl.ds(CX * c + x, 1), :]
            high = y_edge[1, h, pl.ds(CX * c + x, 1), :]
            total = total + jnp.where(row == 0, low, field[h, pl.ds(first - 1, CY), :])
            total = total + jnp.where(row == CY - 1, high, field[h, pl.ds(first + 1, CY), :])
            rows = pl.ds(pl.multiple_of(CX * CY * c + CY * x, 8), CY)
            moved[h, rows, :] = (1.0 - 6.0 * KAPPA) * cells[h] + KAPPA * total
        return carry

    lax.fori_loop(0, CX, column, 0, unroll=8)


def sum_blocks(buffer, count):
    total = buffer[0].astype(F32)
    for n in range(1, count):
        total = total + buffer[n].astype(F32)
    return total


def read_slots(slot_got):
    by = lax.axis_index("by")
    lane = iota((8, 128), 1)
    total = jnp.zeros((8, 128), F32)
    for j in range(BY):
        block = pltpu.roll(slot_got[j], lax.rem(128 + CAP * j - CAP * by, 128), 1)
        total = jnp.where(lane // CAP == j, block, total)
    return total


PAIR, PLANE, LINE, PLANE_ALL, MATE = range(5)


def step_kernel(
    corners_ref, flow_ref, learner_ref, goals_ref, embed_ref, mixer_ref, head_ref,
    moved, full, full_e, head_total, slots,
    field, turned, pieces, order, rows, embed_wide, mixer_wide, embed, mixer, mixer_t, act, slope1,
    slope2, pooled, back, second, first, rows_t, act_t, mixer_early, x_face, y_face, x_halo, y_halo, y_edge,
    head_grad, head_pair, head_got, slot_part, slot_got, own, pair_got, part, plane_got, line_got, part_e, plane_got_e,
    load_sems, weight_sems, halo_send, halo_recv, slot_sems, head_send, head_recv, job_send, job_recv,
):
    bx, by = lax.axis_index("bx"), lax.axis_index("by")
    core = lax.rem(by, 2)
    loads = load_flow(flow_ref, field, load_sems)
    weights = [
        pltpu.make_async_copy(embed_ref, embed_wide, weight_sems.at[0]),
        pltpu.make_async_copy(mixer_ref, mixer_wide, weight_sems.at[1]),
    ]
    for copy in weights:
        copy.start()
    greet()
    make_order(order)
    for h in range(2):
        for c in range(CHAN):
            loads[h * CHAN + c].wait()
        upright(h, field, turned)
    early, late = pl.ds(0, 1024), pl.ds(1024, 1024)

    def product(turned_rows, columns, along, factor):
        return jnp.dot(turned_rows[columns, along], factor[along, :], preferred_element_type=F32)

    cut(range(0, 16), corners_ref, turned, pieces)
    for copy in weights:
        copy.wait()
    order_rows(0, pieces, order, rows, rows_t)
    embed[...] = embed_wide[...].astype(BF16)
    mixer[...] = mixer_wide[...].astype(BF16)
    mixer_t[...] = mixer_wide[...].T.astype(BF16)
    fill_faces(field, x_face, y_face)
    pl.semaphore_wait(pltpu.get_barrier_semaphore(), len(partners()))
    halos = halo_copies(x_face, y_face, x_halo, y_halo, halo_send, halo_recv)
    for copy in halos:
        copy.start()
    for t in range(4):
        forward(t, rows, embed, mixer, act, act_t, slope1, slope2, pooled)
        cut(range(16 + 4 * t, 20 + 4 * t), corners_ref, turned, pieces)
    order_rows(1, pieces, order, rows, rows_t)
    head_step(0, pooled, goals_ref, learner_ref, head_ref, back, head_grad, slot_part)
    for t in range(4, 8):
        forward(t, rows, embed, mixer, act, act_t, slope1, slope2, pooled)
        second_layer_back(t - 4, back, slope2, second)
    head_step(1, pooled, goals_ref, learner_ref, head_ref, back, head_grad, slot_part)
    for half in range(2):
        part_of = pl.ds(256 * half, 256)
        mixer_early[part_of, :] = product(act_t, part_of, early, second)

    send_all("by", lambda peer: slot_part, slot_got.at[by], slot_sems.at[0], slot_sems.at[1])
    slot_got[by] = slot_part[...]
    send_mate(head_grad, head_pair, (head_send.at[0], head_recv.at[0]))

    def head_line(axis, value):
        me = where_am_i()[axis]
        block = head_got.at[axis, me]
        block[...] = value
        send_line(axis, block, (head_send.at[axis + 1], head_recv.at[axis + 1]))

    def head_line_sum(axis):
        wait_all(head_got.at[axis], head_recv.at[axis + 1])
        return sum_blocks(head_got.at[axis], 4)

    def sems(job, group):
        return job_send.at[job, group], job_recv.at[job, group]

    def start_pair(job, gradient):
        own[job] = gradient.reshape(2, 128, HID).astype(BF16)
        send_mate(own.at[job, 1 - core], pair_got.at[job], sems(job, PAIR))

    parts = (part.at[0], part.at[1], part_e)
    gots = (plane_got.at[0], plane_got.at[1], plane_got_e)
    fulls = (full.at[0, core], full.at[1, core], full_e)

    def plane_sends(job):
        me = plane_index(job)
        send_plane(job, lambda n: parts[job].at[n], gots[job].at[me], sems(job, PLANE))
        gots[job][me] = parts[job][me]

    def start_plane(job):
        wait_one(pair_got.at[job], job_recv.at[job, PAIR])
        total = (own[job, core].astype(F32) + pair_got[job].astype(F32)).astype(BF16)
        for n in range(16):
            part[job, n] = total[16 * (n // 2) : 16 * (n // 2) + 16, 256 * (n % 2) : 256 * (n % 2) + 256]
        plane_sends(job)

    def start_plane_e(gradient):
        total = gradient.astype(BF16)
        for n in range(32):
            part_e[n] = total[16 * (n // 2) : 16 * (n // 2) + 16, 256 * (n % 2) : 256 * (n % 2) + 256]
        plane_sends(2)

    def start_line(job):
        wait_all(gots[job], job_recv.at[job, PLANE])
        me = where_am_i()[LINES[job]]
        line_got[job, me] = sum_blocks(gots[job], gots[job].shape[0]).astype(BF16)
        send_line(LINES[job], line_got.at[job, me], sems(job, LINE))

    def start_plane_all(job):
        wait_all(line_got.at[job], job_recv.at[job, LINE])
        block = fulls[job].at[plane_index(job)]
        block[...] = sum_blocks(line_got.at[job], 4).astype(BF16)
        send_plane(job, lambda n: block, block, sems(job, PLANE_ALL))

    def start_mate(job):
        wait_all(fulls[job], job_recv.at[job, PLANE_ALL])
        send_mate(fulls[job], fulls[job], sems(job, MATE))

    for t in range(4, 8):
        second_layer_back(t, back, slope2, second)
    for half in range(2):
        part_of = pl.ds(256 * half, 256)
        start_pair(half, mixer_early[part_of, :] + product(act_t, part_of, late, second))
    for t in range(TILES):
        first_layer_back(t, second, mixer_t, slope1, first)
    start_plane(0)
    start_plane(1)
    start_plane_e(jnp.dot(rows_t[...], first[...], preferred_element_type=F32))

    wait_one(head_pair, head_recv.at[0])
    head_line(1, head_grad[...] + head_pair[...])
    for copy in halos:
        copy.wait()
    place_halos(x_halo, y_halo, field, y_edge)
    start_line(0)
    start_line(1)
    head_line(2, head_line_sum(1))
    diffuse(0, field, y_edge, moved)
    start_plane_all(0)
    start_plane_all(1)
    start_line(2)
    head_line(0, head_line_sum(2))
    diffuse(1, field, y_edge, moved)
    start_plane_all(2)
    wait_all(slot_got, slot_sems.at[1])
    slots[...] = read_slots(slot_got)
    diffuse(2, field, y_edge, moved)
    start_mate(0)
    start_mate(1)
    diffuse(3, field, y_edge, moved)
    head_total[...] = head_line_sum(0)
    wait_all(full_e, job_recv.at[2, PLANE_ALL])
    for job in range(2):
        wait_one(full.at[job, 1 - core], job_recv.at[job, MATE])
    wait_all(slot_got, slot_sems.at[0])
    wait_one(head_pair, head_send.at[0])
    for axis in range(3):
        wait_all(head_got.at[axis], head_send.at[axis + 1])
    for job in range(3):
        wait_all(gots[job], job_send.at[job, PLANE])
        wait_all(line_got.at[job], job_send.at[job, LINE])
        wait_all(fulls[job], job_send.at[job, PLANE_ALL])
    for job in range(2):
        wait_one(pair_got.at[job], job_send.at[job, PAIR])
        wait_one(fulls[job], job_send.at[job, MATE])


def scale_of(square_sum, count):
    return lax.rsqrt(jnp.sum(square_sum, keepdims=True) * (1.0 / count) + EPSILON)


def write_sum(blocks, wide, out, sems):
    total = jnp.zeros((16, 256), F32)
    for block in blocks:
        value = block[...].astype(F32)
        total = total + value * value
    scale = scale_of(total, len(blocks) * 16 * 256)
    copies = []
    for n, block in enumerate(blocks):
        wide[pl.ds(16 * (n // 2), 16), pl.ds(256 * (n % 2), 256)] = block[...].astype(F32) * scale
        if n % 16 == 15:
            rows = pl.ds(128 * (n // 16), 128)
            copies.append(pltpu.make_async_copy(wide.at[rows], out.at[rows], sems.at[n // 16]))
            copies[-1].start()
    return copies


def finish_kernel(
    moved, full, full_e, head_total, slots, flow_out, slot_out, embed_out, mixer_out, head_out,
    embed_wide, mixer_wide, flow_sems, embed_sems, mixer_sems,
):
    copies = []
    for c in range(CHAN):
        part = pl.ds(CX * CY * c, CX * CY)
        for h in range(2):
            copies.append(
                pltpu.make_async_copy(
                    moved.at[h, part], flow_out.at[part, pl.ds(128 * h, 128)], flow_sems.at[h, c]
                )
            )
    for copy in copies:
        copy.start()
    copies += write_sum(
        [full.at[j, h, n] for j in range(2) for h in range(2) for n in range(16)],
        mixer_wide, mixer_out, mixer_sems,
    )
    copies += write_sum([full_e.at[n] for n in range(32)], embed_wide, embed_out, embed_sems)
    total = head_total[...]
    total = total * scale_of(total * total, 3 * HID)
    for k in range(3):
        head_out[k : k + 1, 0:256] = total[k : k + 1]
        head_out[k : k + 1, 256:512] = total[k + 3 : k + 4]
        slot_out[k] = slots[k : k + 1, 0:64]
    for copy in copies:
        copy.wait()


SCRATCH = [
    pltpu.VMEM((2, CHAN * SLAB, 128), F32),
    pltpu.VMEM((CY * CZ + 32, 128), F32),
    pltpu.VMEM((512, 1024), BF16),
    pltpu.VMEM((1024, 1024), BF16),
    pltpu.VMEM((2048, FEAT), BF16),
    pltpu.VMEM((FEAT, HID), F32),
    pltpu.VMEM((HID, HID), F32),
    pltpu.VMEM((FEAT, HID), BF16),
    pltpu.VMEM((HID, HID), BF16),
    pltpu.VMEM((HID, HID), BF16),
    pltpu.VMEM((2048, HID), BF16),
    pltpu.VMEM((2048, HID), F32),
    pltpu.VMEM((2048, HID), F32),
    pltpu.VMEM((TILES, 4, HID), F32),
    pltpu.VMEM((TILES, 4, HID), F32),
    pltpu.VMEM((2048, HID), BF16),
    pltpu.VMEM((2048, HID), BF16),
    pltpu.VMEM((FEAT, 2048), BF16),
    pltpu.VMEM((HID, 2048), BF16),
    pltpu.VMEM((HID, HID), F32),
    pltpu.VMEM((2, 2, CHAN * CY, 128), BF16),
    pltpu.VMEM((2, 2, CHAN * CX, 128), BF16),
    pltpu.VMEM((2, 2, CHAN * CY, 128), BF16),
    pltpu.VMEM((2, 2, CHAN * CX, 128), BF16),
    pltpu.VMEM((2, 2, CHAN * CX, 128), F32),
    pltpu.VMEM((8, 256), F32),
    pltpu.VMEM((8, 256), F32),
    pltpu.VMEM((3, 4, 8, 256), F32),
    pltpu.VMEM((8, 128), F32),
    pltpu.VMEM((BY, 8, 128), F32),
    pltpu.VMEM((2, 2, 128, HID), BF16),
    pltpu.VMEM((2, 128, HID), BF16),
    pltpu.VMEM((2, 16, 16, 256), BF16),
    pltpu.VMEM((2, 16, 16, 256), BF16),
    pltpu.VMEM((3, 4, 16, 256), BF16),
    pltpu.VMEM((32, 16, 256), BF16),
    pltpu.VMEM((32, 16, 256), BF16),
    pltpu.SemaphoreType.DMA((2, CHAN)),
    pltpu.SemaphoreType.DMA((2,)),
    pltpu.SemaphoreType.DMA((4,)),
    pltpu.SemaphoreType.DMA((4,)),
    pltpu.SemaphoreType.DMA((2,)),
    pltpu.SemaphoreType.DMA((4,)),
    pltpu.SemaphoreType.DMA((4,)),
    pltpu.SemaphoreType.DMA((3, 5)),
    pltpu.SemaphoreType.DMA((3, 5)),
]


def per_device(
    flow_field, patch_corners, patch_learner, drag_target, embed_weight, mixer_weight, head_weight
):
    vmem = pl.BlockSpec(memory_space=pltpu.VMEM)
    anywhere = pl.BlockSpec(memory_space=pl.ANY)
    parts = pl.pallas_call(
        step_kernel,
        out_shape=(
            pltpu.VMEM((2, COLS, 128), F32),
            pltpu.VMEM((2, 2, 16, 16, 256), BF16),
            pltpu.VMEM((32, 16, 256), BF16),
            pltpu.VMEM((8, 256), F32),
            pltpu.VMEM((8, 128), F32),
        ),
        in_specs=[pl.BlockSpec(memory_space=pltpu.SMEM), anywhere, vmem, vmem, anywhere, anywhere, vmem],
        out_specs=(vmem,) * 5,
        scratch_shapes=SCRATCH,
        compiler_params=pltpu.CompilerParams(
            collective_id=0, has_side_effects=True, vmem_limit_bytes=44 * 2**20
        ),
    )(
        *(
            pltpu.with_memory_space_constraint(value, pltpu.HBM)
            for value in (
                patch_corners, flow_field.reshape(COLS, CZ), patch_learner.reshape(1, PB),
                drag_target.reshape(3, PB), embed_weight, mixer_weight, head_weight,
            )
        )
    )
    flow, slots, embed, mixer, head = pl.pallas_call(
        finish_kernel,
        out_shape=(
            jax.ShapeDtypeStruct((COLS, CZ), F32),
            jax.ShapeDtypeStruct((3, 1, 64), F32),
            jax.ShapeDtypeStruct((FEAT, HID), F32),
            jax.ShapeDtypeStruct((HID, HID), F32),
            jax.ShapeDtypeStruct((3, HID), F32),
        ),
        in_specs=[vmem] * 5,
        out_specs=(anywhere, vmem, anywhere, anywhere, vmem),
        scratch_shapes=[
            pltpu.VMEM((FEAT, HID), F32),
            pltpu.VMEM((HID, HID), F32),
            pltpu.SemaphoreType.DMA((2, CHAN)),
            pltpu.SemaphoreType.DMA((2,)),
            pltpu.SemaphoreType.DMA((4,)),
        ],
        compiler_params=pltpu.CompilerParams(vmem_limit_bytes=16 * 2**20),
    )(*parts)
    return flow.reshape(CHAN, CX, CY, CZ), slots, embed, mixer, head


def solution(mesh):
    return jax.shard_map(
        per_device,
        mesh=mesh,
        in_specs=(
            P(None, "bx", "by", None),
            P(None, "bx", "by"),
            P("bx", "by", None),
            P(None, "bx", "by"),
            P(),
            P(),
            P(),
        ),
        out_specs=(P(None, "bx", "by", None), P(None, "bx", "by"), P(), P(), P()),
        check_vma=False,
    )
```

time: 410 us -> 42.9 us (0.10)
  local copies, waits for them, and re-layouts: 151 us -> 0 us
  waiting for transfers between devices: 82.9 us -> 0 us
  blocking collectives: 67.6 us -> 0 us
  Pallas kernels: 0 us -> 41.9 us
  matrix products: 35.7 us -> 0 us
  other arithmetic: 31.4 us -> 0 us
  starting transfers between devices: 21.8 us -> 0 us
  between operations: 16.3 us -> 0.8 us
    gather x97 -> x0, local copies, waits for them, and re-layouts: 125 us -> none
    psum x1 -> x0, waiting for transfers between devices: 73.7 us -> none  [per_device(): lax.psum((grad_embed, grad_mixer, grad_head), ('bx', 'by'))]
    psum x1 -> x0, blocking collectives: 67.6 us -> none  [per_device(): lax.psum((grad_embed, grad_mixer, grad_head), ('bx', 'by'))]
    pallas_call x0 -> x2, Pallas kernels: none -> 41.9 us  [the longest x1 38.9 us: per_device(): pl.pallas_call(step_kernel, out_shape=(pltpu.VMEM((2, COLS, 128), F32), p...]
    dot_general x9 -> x0, matrix products: 35.7 us -> none  [the longest x1 13.8 us: closure_grads(): lax.dot_general(inputs, first_grad, (((0,), (0,)), ((), ())), preferred_e...]
    all_to_all x2 -> x0, starting transfers between devices: 16.6 us -> none  [the longest x1 9.3 us: per_device(): lax.all_to_all(sent_goals, 'by', split_axis=0, concat_axis=0, tiled=True)]
    convert_element_type x6 -> x0, other arithmetic: 10.6 us -> none  [the longest x1 6.71 us: closure_grads(): second_back.reshape(count * per_patch, hidden).astype(jnp.bfloat16)]
    slice x4 -> x0, local copies, waits for them, and re-layouts: 9.89 us -> none  [the longest x1 3.29 us: diffuse_local(): flow_field[:, :, 1:]]
  transfers between devices with their start and end apart: 7 -> 0, of which waited for: 3 -> 0; matrix products, arithmetic and copies ran while one was open for 39% -> 0% of each run, Pallas kernels for 0% -> 0%
where the time goes in v1:
time: 42.9 us; the launch traced here: 42.7 us
  Pallas kernels  41.9 us (98%)
  between operations  0.8 us (2%)
    pallas_call x1, Pallas kernels, per_device(): pl.pallas_call(step_kernel, out_shape=(pltpu.VMEM((2, COLS, 128), F32), p...  38.9 us
    pallas_call x1, Pallas kernels, per_device(): pl.pallas_call(finish_kernel, out_shape=(jax.ShapeDtypeStruct((COLS, CZ),...  3.02 us

profile of v1, /device:TPU:1, one launch (start us, length us, event | category | flops | bytes accessed | tf_op | source)
XLA Modules:
  0.0 42.7 jit_solution(16026161209632894176)
XLA Ops:
  0.6 38.9 %shard_map.110 = (f32[2,3072,128]{2,1,0:T(8,128)S(1)}, bf16[2,2,16,16,256]{4,3,2,1,0:T(8,128)(2,1)S(1)}, bf16[32,16,256]{2,1,0:T(8,128)(2,1)S(1)}, f32[8,256]{1,0:T(8,128)S(1)}, f32[8,128]{1,0:T(8,128)S(1)}) custom-call(s32[3,1,32]{2,1,0:T(1,128)} %corners_ref.1, f32[3072,256]{1,0:T(8,128)} %bitcast.4, s32[1,32]{1,0:T(1,128)} %bitcast.6, ...), custom_call_target="tpu_custom_call" | custom-call | tf_op jit(solution)/shard_map/pallas_call | solution.py:670
  39.5 3.0 %shard_map.111 = (f32[3072,256]{1,0:T(8,128)}, f32[3,1,64]{2,1,0:T(1,128)}, f32[256,512]{1,0:T(8,128)}, f32[512,512]{1,0:T(8,128)}, f32[3,512]{1,0:T(4,128)}) custom-call(f32[2,3072,128]{2,1,0:T(8,128)S(1)} %get-tuple-element.15.moved, bf16[2,2,16,16,256]{4,3,2,1,0:T(8,128)(2,1)S(1)} %get-tuple-element.16.full, ...), custom_call_target="tpu_custom_call" | custom-call | tf_op jit(solution)/shard_map/pallas_call | solution.py:694

commit v2 on v1

--- a/solution.py
+++ b/solution.py
@@ -33,16 +33,18 @@
 
 
 def load_flow(flow_ref, field, sems):
-    copies = [
-        pltpu.make_async_copy(
-            flow_ref.at[pl.ds(CX * CY * c, CX * CY), pl.ds(128 * h, 128)],
-            field.at[h, pl.ds(SLAB * c + CY, CX * CY)],
-            sems.at[h, c],
+    cells = field.reshape(2, CHAN * (CX + 2), CY, 128)
+
+    def copy(block, h, c):
+        levels = pl.ds(8 * block, 8)
+        return pltpu.make_async_copy(
+            flow_ref.at[pl.ds(CX * c, CX), levels, pl.ds(128 * h, 128)],
+            cells.at[h, pl.ds((CX + 2) * c + 1, CX), levels],
+            sems.at[block, h, c],
         )
-        for h in range(2)
-        for c in range(CHAN)
-    ]
-    for copy in copies:
+
+    copies = [[[copy(block, h, c) for c in range(CHAN)] for h in range(2)] for block in range(3)]
+    for copy in sum(sum(copies, []), []):
         copy.start()
     return copies
 
@@ -53,8 +55,8 @@
     )
 
 
-def upright(h, field, turned):
-    for y in range(CY):
+def upright(block, h, field, turned):
+    for y in range(8 * block, 8 * block + 8):
         turned[pl.ds(y * CZ + 128 * h, 128), :] = level_of(field, h, y).T
 
 
@@ -375,7 +377,7 @@
             total = total + jnp.where(row == 0, low, field[h, pl.ds(first - 1, CY), :])
             total = total + jnp.where(row == CY - 1, high, field[h, pl.ds(first + 1, CY), :])
             rows = pl.ds(pl.multiple_of(CX * CY * c + CY * x, 8), CY)
-            moved[h, rows, :] = (1.0 - 6.0 * KAPPA) * cells[h] + KAPPA * total
+            moved[rows, pl.ds(128 * h, 128)] = (1.0 - 6.0 * KAPPA) * cells[h] + KAPPA * total
         return carry
 
     lax.fori_loop(0, CX, column, 0, unroll=8)
@@ -420,10 +422,11 @@
         copy.start()
     greet()
     make_order(order)
-    for h in range(2):
-        for c in range(CHAN):
-            loads[h * CHAN + c].wait()
-        upright(h, field, turned)
+    for block in range(3):
+        for h in range(2):
+            for copy in loads[block][h]:
+                copy.wait()
+            upright(block, h, field, turned)
     early, late = pl.ds(0, 1024), pl.ds(1024, 1024)
 
     def product(turned_rows, columns, along, factor):
@@ -587,14 +590,9 @@
     embed_wide, mixer_wide, flow_sems, embed_sems, mixer_sems,
 ):
     copies = []
-    for c in range(CHAN):
-        part = pl.ds(CX * CY * c, CX * CY)
-        for h in range(2):
-            copies.append(
-                pltpu.make_async_copy(
-                    moved.at[h, part], flow_out.at[part, pl.ds(128 * h, 128)], flow_sems.at[h, c]
-                )
-            )
+    for n in range(8):
+        part = pl.ds(COLS // 8 * n, COLS // 8)
+        copies.append(pltpu.make_async_copy(moved.at[part], flow_out.at[part], flow_sems.at[n]))
     for copy in copies:
         copy.start()
     copies += write_sum(
@@ -650,7 +648,7 @@
     pltpu.VMEM((3, 4, 16, 256), BF16),
     pltpu.VMEM((32, 16, 256), BF16),
     pltpu.VMEM((32, 16, 256), BF16),
-    pltpu.SemaphoreType.DMA((2, CHAN)),
+    pltpu.SemaphoreType.DMA((3, 2, CHAN)),
     pltpu.SemaphoreType.DMA((2,)),
     pltpu.SemaphoreType.DMA((4,)),
     pltpu.SemaphoreType.DMA((4,)),
@@ -670,7 +668,7 @@
     parts = pl.pallas_call(
         step_kernel,
         out_shape=(
-            pltpu.VMEM((2, COLS, 128), F32),
+            pltpu.VMEM((COLS, CZ), F32),
             pltpu.VMEM((2, 2, 16, 16, 256), BF16),
             pltpu.VMEM((32, 16, 256), BF16),
             pltpu.VMEM((8, 256), F32),
@@ -686,7 +684,7 @@
         *(
             pltpu.with_memory_space_constraint(value, pltpu.HBM)
             for value in (
-                patch_corners, flow_field.reshape(COLS, CZ), patch_learner.reshape(1, PB),
+                patch_corners, flow_field.reshape(CHAN * CX, CY, CZ), patch_learner.reshape(1, PB),
                 drag_target.reshape(3, PB), embed_weight, mixer_weight, head_weight,
             )
         )
@@ -705,7 +703,7 @@
         scratch_shapes=[
             pltpu.VMEM((FEAT, HID), F32),
             pltpu.VMEM((HID, HID), F32),
-            pltpu.SemaphoreType.DMA((2, CHAN)),
+            pltpu.SemaphoreType.DMA((8,)),
             pltpu.SemaphoreType.DMA((2,)),
             pltpu.SemaphoreType.DMA((4,)),
         ],

time: 42.9 us -> 43 us (level)
  no operation moved by 1% of the time
where the time goes in v2:
time: 43 us; the launch traced here: 42.8 us
  Pallas kernels  42 us (98%)
  between operations  0.8 us (2%)
    pallas_call x1, Pallas kernels, per_device(): pl.pallas_call(step_kernel, out_shape=(pltpu.VMEM((COLS, CZ), F32), pltpu...  39.1 us
    pallas_call x1, Pallas kernels, per_device(): pl.pallas_call(finish_kernel, out_shape=(jax.ShapeDtypeStruct((COLS, CZ),...  2.92 us

profile of v2, /device:TPU:1, one launch (start us, length us, event | category | flops | bytes accessed | tf_op | source)
XLA Modules:
  0.0 42.8 jit_solution(12964242465898928129)
XLA Ops:
  0.6 39.1 %shard_map.110 = (f32[3072,256]{1,0:T(8,128)S(1)}, bf16[2,2,16,16,256]{4,3,2,1,0:T(8,128)(2,1)S(1)}, bf16[32,16,256]{2,1,0:T(8,128)(2,1)S(1)}, f32[8,256]{1,0:T(8,128)S(1)}, f32[8,128]{1,0:T(8,128)S(1)}) custom-call(s32[3,1,32]{2,1,0:T(1,128)} %corners_ref.1, f32[128,24,256]{2,1,0:T(8,128)} %bitcast.4, s32[1,32]{1,0:T(1,128)} %bitcast.6, ...), custom_call_target="tpu_custom_call" | custom-call | tf_op jit(solution)/shard_map/pallas_call | solution.py:668
  39.8 2.9 %shard_map.111 = (f32[3072,256]{1,0:T(8,128)}, f32[3,1,64]{2,1,0:T(1,128)}, f32[256,512]{1,0:T(8,128)}, f32[512,512]{1,0:T(8,128)}, f32[3,512]{1,0:T(4,128)}) custom-call(f32[3072,256]{1,0:T(8,128)S(1)} %get-tuple-element.15.moved, bf16[2,2,16,16,256]{4,3,2,1,0:T(8,128)(2,1)S(1)} %get-tuple-element.16.full, ...), custom_call_target="tpu_custom_call" | custom-call | tf_op jit(solution)/shard_map/pallas_call | solution.py:692

commit v3 on v2

--- a/solution.py
+++ b/solution.py
@@ -404,9 +404,9 @@
 
 
 def step_kernel(
-    corners_ref, flow_ref, learner_ref, goals_ref, embed_ref, mixer_ref, head_ref,
+    corners_in, flow_ref, learner_in, goals_in, embed_ref, mixer_ref, head_in,
     moved, full, full_e, head_total, slots,
-    field, turned, pieces, order, rows, embed_wide, mixer_wide, embed, mixer, mixer_t, act, slope1,
+    corners_ref, learner_ref, goals_ref, head_ref, field, turned, pieces, order, rows, embed_wide, mixer_wide, embed, mixer, mixer_t, act, slope1,
     slope2, pooled, back, second, first, rows_t, act_t, mixer_early, x_face, y_face, x_halo, y_halo, y_edge,
     head_grad, head_pair, head_got, slot_part, slot_got, own, pair_got, part, plane_got, line_got, part_e, plane_got_e,
     load_sems, weight_sems, halo_send, halo_recv, slot_sems, head_send, head_recv, job_send, job_recv,
@@ -414,9 +414,16 @@
     bx, by = lax.axis_index("bx"), lax.axis_index("by")
     core = lax.rem(by, 2)
     loads = load_flow(flow_ref, field, load_sems)
+    corners = pltpu.make_async_copy(corners_in, corners_ref, weight_sems.at[0])
+    corners.start()
     weights = [
-        pltpu.make_async_copy(embed_ref, embed_wide, weight_sems.at[0]),
-        pltpu.make_async_copy(mixer_ref, mixer_wide, weight_sems.at[1]),
+        pltpu.make_async_copy(source, target, weight_sems.at[n + 1])
+        for n, (source, target) in enumerate(
+            (
+                (embed_ref, embed_wide), (mixer_ref, mixer_wide), (learner_in, learner_ref),
+                (goals_in, goals_ref), (head_in, head_ref),
+            )
+        )
     ]
     for copy in weights:
         copy.start()
@@ -432,6 +439,7 @@
     def product(turned_rows, columns, along, factor):
         return jnp.dot(turned_rows[columns, along], factor[along, :], preferred_element_type=F32)
 
+    corners.wait()
     cut(range(0, 16), corners_ref, turned, pieces)
     for copy in weights:
         copy.wait()
@@ -587,7 +595,7 @@
 
 def finish_kernel(
     moved, full, full_e, head_total, slots, flow_out, slot_out, embed_out, mixer_out, head_out,
-    embed_wide, mixer_wide, flow_sems, embed_sems, mixer_sems,
+    slot_wide, head_wide, embed_wide, mixer_wide, flow_sems, small_sems, embed_sems, mixer_sems,
 ):
     copies = []
     for n in range(8):
@@ -595,22 +603,29 @@
         copies.append(pltpu.make_async_copy(moved.at[part], flow_out.at[part], flow_sems.at[n]))
     for copy in copies:
         copy.start()
+    total = head_total[...]
+    total = total * scale_of(total * total, 3 * HID)
+    for k in range(3):
+        head_wide[k : k + 1, 0:256] = total[k : k + 1]
+        head_wide[k : k + 1, 256:512] = total[k + 3 : k + 4]
+        slot_wide[k] = slots[k : k + 1, 0:64]
+    for n, (source, target) in enumerate(((slot_wide, slot_out), (head_wide, head_out))):
+        copies.append(pltpu.make_async_copy(source, target, small_sems.at[n]))
+        copies[-1].start()
     copies += write_sum(
         [full.at[j, h, n] for j in range(2) for h in range(2) for n in range(16)],
         mixer_wide, mixer_out, mixer_sems,
     )
     copies += write_sum([full_e.at[n] for n in range(32)], embed_wide, embed_out, embed_sems)
-    total = head_total[...]
-    total = total * scale_of(total * total, 3 * HID)
-    for k in range(3):
-        head_out[k : k + 1, 0:256] = total[k : k + 1]
-        head_out[k : k + 1, 256:512] = total[k + 3 : k + 4]
-        slot_out[k] = slots[k : k + 1, 0:64]
     for copy in copies:
         copy.wait()
 
 
 SCRATCH = [
+    pltpu.SMEM((3, 1, PB), jnp.int32),
+    pltpu.VMEM((1, PB), jnp.int32),
+    pltpu.VMEM((3, PB), BF16),
+    pltpu.VMEM((3, HID), F32),
     pltpu.VMEM((2, CHAN * SLAB, 128), F32),
     pltpu.VMEM((CY * CZ + 32, 128), F32),
     pltpu.VMEM((512, 1024), BF16),
@@ -649,7 +664,7 @@
     pltpu.VMEM((32, 16, 256), BF16),
     pltpu.VMEM((32, 16, 256), BF16),
     pltpu.SemaphoreType.DMA((3, 2, CHAN)),
-    pltpu.SemaphoreType.DMA((2,)),
+    pltpu.SemaphoreType.DMA((6,)),
     pltpu.SemaphoreType.DMA((4,)),
     pltpu.SemaphoreType.DMA((4,)),
     pltpu.SemaphoreType.DMA((2,)),
@@ -674,7 +689,7 @@
             pltpu.VMEM((8, 256), F32),
             pltpu.VMEM((8, 128), F32),
         ),
-        in_specs=[pl.BlockSpec(memory_space=pltpu.SMEM), anywhere, vmem, vmem, anywhere, anywhere, vmem],
+        in_specs=[anywhere] * 7,
         out_specs=(vmem,) * 5,
         scratch_shapes=SCRATCH,
         compiler_params=pltpu.CompilerParams(
@@ -699,11 +714,14 @@
             jax.ShapeDtypeStruct((3, HID), F32),
         ),
         in_specs=[vmem] * 5,
-        out_specs=(anywhere, vmem, anywhere, anywhere, vmem),
+        out_specs=(anywhere,) * 5,
         scratch_shapes=[
+            pltpu.VMEM((3, 1, 64), F32),
+            pltpu.VMEM((3, HID), F32),
             pltpu.VMEM((FEAT, HID), F32),
             pltpu.VMEM((HID, HID), F32),
             pltpu.SemaphoreType.DMA((8,)),
+            pltpu.SemaphoreType.DMA((2,)),
             pltpu.SemaphoreType.DMA((2,)),
             pltpu.SemaphoreType.DMA((4,)),
         ],

time: 43 us -> 41.6 us (0.967)
  Pallas kernels: 42 us -> 40.6 us
    pallas_call x1, Pallas kernels: 39.1 us -> 38.3 us  [per_device(): pl.pallas_call(step_kernel, out_shape=(pltpu.VMEM((COLS, CZ), F32), pltpu...]
    pallas_call x1, Pallas kernels: 2.92 us -> 2.31 us  [per_device(): pl.pallas_call(finish_kernel, out_shape=(jax.ShapeDtypeStruct((COLS, CZ),...]
where the time goes in v3:
time: 41.6 us; the launch traced here: 41.5 us
  Pallas kernels  40.6 us (98%)
  between operations  0.8 us (2%)
    pallas_call x1, Pallas kernels, per_device(): pl.pallas_call(step_kernel, out_shape=(pltpu.VMEM((COLS, CZ), F32), pltpu...  38.3 us
    pallas_call x1, Pallas kernels, per_device(): pl.pallas_call(finish_kernel, out_shape=(jax.ShapeDtypeStruct((COLS, CZ),...  2.31 us

profile of v3, /device:TPU:1, one launch (start us, length us, event | category | flops | bytes accessed | tf_op | source)
XLA Modules:
  0.0 41.5 jit_solution(14509510392765806426)
XLA Ops:
  0.6 38.3 %shard_map.110 = (f32[3072,256]{1,0:T(8,128)S(1)}, bf16[2,2,16,16,256]{4,3,2,1,0:T(8,128)(2,1)S(1)}, bf16[32,16,256]{2,1,0:T(8,128)(2,1)S(1)}, f32[8,256]{1,0:T(8,128)S(1)}, f32[8,128]{1,0:T(8,128)S(1)}) custom-call(s32[3,1,32]{2,1,0:T(1,128)} %corners_in.1, f32[128,24,256]{2,1,0:T(8,128)} %bitcast.4, s32[1,32]{1,0:T(1,128)} %bitcast.6, ...), custom_call_target="tpu_custom_call" | custom-call | tf_op jit(solution)/shard_map/pallas_call | solution.py:683
  39.0 2.3 %shard_map.111 = (f32[3072,256]{1,0:T(8,128)}, f32[3,1,64]{2,1,0:T(1,128)}, f32[256,512]{1,0:T(8,128)}, f32[512,512]{1,0:T(8,128)}, f32[3,512]{1,0:T(4,128)}) custom-call(f32[3072,256]{1,0:T(8,128)S(1)} %get-tuple-element.15.moved, bf16[2,2,16,16,256]{4,3,2,1,0:T(8,128)(2,1)S(1)} %get-tuple-element.16.full, ...), custom_call_target="tpu_custom_call" | custom-call | tf_op jit(solution)/shard_map/pallas_call | solution.py:707

commit v4 on v3

--- a/solution.py
+++ b/solution.py
@@ -13,6 +13,7 @@
 BX, BY = 8, 16
 MESH = pl.DeviceIdType.MESH
 TILES = 8
+EARLY = 6
 KAPPA = 0.15
 EPSILON = 1e-06
 GELU_S = 0.7978845608028654
@@ -126,10 +127,9 @@
         pooled[t, :, columns] = value * (1.0 / 64)
 
 
-def head_step(half, pooled_ref, goals_ref, learner_ref, head_ref, back, head_grad, slot_part):
-    some = PB // 2
-    first = some * half
-    pooled = pooled_ref[pl.ds(4 * half, 4)].reshape(some, HID)
+def head_step(tiles, pooled_ref, goals_ref, learner_ref, head_ref, back, head_grad, slot_part):
+    some, first = 4 * len(tiles), 4 * tiles[0]
+    pooled = pooled_ref[pl.ds(tiles[0], len(tiles))].reshape(some, HID)
     head = head_ref[...]
     patch = iota((some, PB), 0) + first
     other = iota((some, PB), 1)
@@ -150,8 +150,8 @@
         total = total + misfit * weight
         head_rows.append(jnp.sum(misfit * pooled, axis=0, keepdims=True))
         slot_rows.append(jnp.sum(jnp.where(place, predicted, 0.0), axis=0, keepdims=True))
-    back[pl.ds(4 * half, 4)] = (total * (1.0 / 64)).reshape(4, 4, HID)
-    if half == 0:
+    back[pl.ds(tiles[0], len(tiles))] = (total * (1.0 / 64)).reshape(len(tiles), 4, HID)
+    if first == 0:
         head_grad[...] = jnp.zeros_like(head_grad)
         slot_part[...] = jnp.zeros_like(slot_part)
     for k in range(3):
@@ -434,7 +434,7 @@
             for copy in loads[block][h]:
                 copy.wait()
             upright(block, h, field, turned)
-    early, late = pl.ds(0, 1024), pl.ds(1024, 1024)
+    early, late = pl.ds(0, 256 * EARLY), pl.ds(256 * EARLY, 256 * (TILES - EARLY))
 
     def product(turned_rows, columns, along, factor):
         return jnp.dot(turned_rows[columns, along], factor[along, :], preferred_element_type=F32)
@@ -456,17 +456,18 @@
         forward(t, rows, embed, mixer, act, act_t, slope1, slope2, pooled)
         cut(range(16 + 4 * t, 20 + 4 * t), corners_ref, turned, pieces)
     order_rows(1, pieces, order, rows, rows_t)
-    head_step(0, pooled, goals_ref, learner_ref, head_ref, back, head_grad, slot_part)
-    for t in range(4, 8):
+    for t in range(4, TILES):
         forward(t, rows, embed, mixer, act, act_t, slope1, slope2, pooled)
-        second_layer_back(t - 4, back, slope2, second)
-    head_step(1, pooled, goals_ref, learner_ref, head_ref, back, head_grad, slot_part)
+        if t == EARLY - 1:
+            head_step(range(EARLY), pooled, goals_ref, learner_ref, head_ref, back, head_grad, slot_part)
+        if t >= EARLY:
+            for n in range(3 * (t - EARLY), 3 * (t - EARLY) + 3):
+                second_layer_back(n, back, slope2, second)
+    head_step(range(EARLY, TILES), pooled, goals_ref, learner_ref, head_ref, back, head_grad, slot_part)
     for half in range(2):
         part_of = pl.ds(256 * half, 256)
         mixer_early[part_of, :] = product(act_t, part_of, early, second)
 
-    send_all("by", lambda peer: slot_part, slot_got.at[by], slot_sems.at[0], slot_sems.at[1])
-    slot_got[by] = slot_part[...]
     send_mate(head_grad, head_pair, (head_send.at[0], head_recv.at[0]))
 
     def head_line(axis, value):
@@ -524,7 +525,7 @@
         wait_all(fulls[job], job_recv.at[job, PLANE_ALL])
         send_mate(fulls[job], fulls[job], sems(job, MATE))
 
-    for t in range(4, 8):
+    for t in range(EARLY, TILES):
         second_layer_back(t, back, slope2, second)
     for half in range(2):
         part_of = pl.ds(256 * half, 256)
@@ -543,6 +544,8 @@
     start_line(0)
     start_line(1)
     head_line(2, head_line_sum(1))
+    send_all("by", lambda peer: slot_part, slot_got.at[by], slot_sems.at[0], slot_sems.at[1])
+    slot_got[by] = slot_part[...]
     diffuse(0, field, y_edge, moved)
     start_plane_all(0)
     start_plane_all(1)

time: 41.6 us -> 42.2 us (1.014)
  Pallas kernels: 40.6 us -> 41.4 us
    pallas_call x1, Pallas kernels: 38.3 us -> 39.1 us  [per_device(): pl.pallas_call(step_kernel, out_shape=(pltpu.VMEM((COLS, CZ), F32), pltpu...]
where the time goes in v4:
time: 42.2 us; the launch traced here: 42.1 us
  Pallas kernels  41.4 us (98%)
  between operations  0.64 us (2%)
    pallas_call x1, Pallas kernels, per_device(): pl.pallas_call(step_kernel, out_shape=(pltpu.VMEM((COLS, CZ), F32), pltpu...  39.1 us
    pallas_call x1, Pallas kernels, per_device(): pl.pallas_call(finish_kernel, out_shape=(jax.ShapeDtypeStruct((COLS, CZ),...  2.31 us

profile of v4, /device:TPU:1, one launch (start us, length us, event | category | flops | bytes accessed | tf_op | source)
XLA Modules:
  0.0 42.1 jit_solution(16768520956880586400)
XLA Ops:
  0.6 39.1 %shard_map.110 = (f32[3072,256]{1,0:T(8,128)S(1)}, bf16[2,2,16,16,256]{4,3,2,1,0:T(8,128)(2,1)S(1)}, bf16[32,16,256]{2,1,0:T(8,128)(2,1)S(1)}, f32[8,256]{1,0:T(8,128)S(1)}, f32[8,128]{1,0:T(8,128)S(1)}) custom-call(s32[3,1,32]{2,1,0:T(1,128)} %corners_in.1, f32[128,24,256]{2,1,0:T(8,128)} %bitcast.4, s32[1,32]{1,0:T(1,128)} %bitcast.6, ...), custom_call_target="tpu_custom_call" | custom-call | tf_op jit(solution)/shard_map/pallas_call | solution.py:686
  39.8 2.3 %shard_map.111 = (f32[3072,256]{1,0:T(8,128)}, f32[3,1,64]{2,1,0:T(1,128)}, f32[256,512]{1,0:T(8,128)}, f32[512,512]{1,0:T(8,128)}, f32[3,512]{1,0:T(4,128)}) custom-call(f32[3072,256]{1,0:T(8,128)S(1)} %get-tuple-element.15.moved, bf16[2,2,16,16,256]{4,3,2,1,0:T(8,128)(2,1)S(1)} %get-tuple-element.16.full, ...), custom_call_target="tpu_custom_call" | custom-call | tf_op jit(solution)/shard_map/pallas_call | solution.py:710

commit v5 on v4

--- a/solution.py
+++ b/solution.py
@@ -407,7 +407,7 @@
     corners_in, flow_ref, learner_in, goals_in, embed_ref, mixer_ref, head_in,
     moved, full, full_e, head_total, slots,
     corners_ref, learner_ref, goals_ref, head_ref, field, turned, pieces, order, rows, embed_wide, mixer_wide, embed, mixer, mixer_t, act, slope1,
-    slope2, pooled, back, second, first, rows_t, act_t, mixer_early, x_face, y_face, x_halo, y_halo, y_edge,
+    slope2, pooled, back, second, first, rows_t, act_t, mixer_early, embed_early, x_face, y_face, x_halo, y_halo, y_edge,
     head_grad, head_pair, head_got, slot_part, slot_got, own, pair_got, part, plane_got, line_got, part_e, plane_got_e,
     load_sems, weight_sems, halo_send, halo_recv, slot_sems, head_send, head_recv, job_send, job_recv,
 ):
@@ -463,10 +463,12 @@
         if t >= EARLY:
             for n in range(3 * (t - EARLY), 3 * (t - EARLY) + 3):
                 second_layer_back(n, back, slope2, second)
+                first_layer_back(n, second, mixer_t, slope1, first)
     head_step(range(EARLY, TILES), pooled, goals_ref, learner_ref, head_ref, back, head_grad, slot_part)
     for half in range(2):
         part_of = pl.ds(256 * half, 256)
         mixer_early[part_of, :] = product(act_t, part_of, early, second)
+    embed_early[...] = product(rows_t, pl.ds(0, FEAT), early, first)
 
     send_mate(head_grad, head_pair, (head_send.at[0], head_recv.at[0]))
 
@@ -530,11 +532,11 @@
     for half in range(2):
         part_of = pl.ds(256 * half, 256)
         start_pair(half, mixer_early[part_of, :] + product(act_t, part_of, late, second))
-    for t in range(TILES):
+    for t in range(EARLY, TILES):
         first_layer_back(t, second, mixer_t, slope1, first)
+    start_plane_e(embed_early[...] + product(rows_t, pl.ds(0, FEAT), late, first))
     start_plane(0)
     start_plane(1)
-    start_plane_e(jnp.dot(rows_t[...], first[...], preferred_element_type=F32))
 
     wait_one(head_pair, head_recv.at[0])
     head_line(1, head_grad[...] + head_pair[...])
@@ -649,6 +651,7 @@
     pltpu.VMEM((FEAT, 2048), BF16),
     pltpu.VMEM((HID, 2048), BF16),
     pltpu.VMEM((HID, HID), F32),
+    pltpu.VMEM((FEAT, HID), F32),
     pltpu.VMEM((2, 2, CHAN * CY, 128), BF16),
     pltpu.VMEM((2, 2, CHAN * CX, 128), BF16),
     pltpu.VMEM((2, 2, CHAN * CY, 128), BF16),

time: 42.2 us -> 42.9 us (1.017)
  Pallas kernels: 41.4 us -> 42.2 us
    pallas_call x1, Pallas kernels: 39.1 us -> 39.9 us  [per_device(): pl.pallas_call(step_kernel, out_shape=(pltpu.VMEM((COLS, CZ), F32), pltpu...]
where the time goes in v5:
time: 42.9 us; the launch traced here: 42.8 us
  Pallas kernels  42.2 us (98%)
  between operations  0.64 us (1%)
    pallas_call x1, Pallas kernels, per_device(): pl.pallas_call(step_kernel, out_shape=(pltpu.VMEM((COLS, CZ), F32), pltpu...  39.9 us
    pallas_call x1, Pallas kernels, per_device(): pl.pallas_call(finish_kernel, out_shape=(jax.ShapeDtypeStruct((COLS, CZ),...  2.31 us

profile of v5, /device:TPU:1, one launch (start us, length us, event | category | flops | bytes accessed | tf_op | source)
XLA Modules:
  0.0 42.8 jit_solution(18228716218775918669)
XLA Ops:
  0.6 39.9 %shard_map.110 = (f32[3072,256]{1,0:T(8,128)S(1)}, bf16[2,2,16,16,256]{4,3,2,1,0:T(8,128)(2,1)S(1)}, bf16[32,16,256]{2,1,0:T(8,128)(2,1)S(1)}, f32[8,256]{1,0:T(8,128)S(1)}, f32[8,128]{1,0:T(8,128)S(1)}) custom-call(s32[3,1,32]{2,1,0:T(1,128)} %corners_in.1, f32[128,24,256]{2,1,0:T(8,128)} %bitcast.4, s32[1,32]{1,0:T(1,128)} %bitcast.6, ...), custom_call_target="tpu_custom_call" | custom-call | tf_op jit(solution)/shard_map/pallas_call | solution.py:689
  40.5 2.3 %shard_map.111 = (f32[3072,256]{1,0:T(8,128)}, f32[3,1,64]{2,1,0:T(1,128)}, f32[256,512]{1,0:T(8,128)}, f32[512,512]{1,0:T(8,128)}, f32[3,512]{1,0:T(4,128)}) custom-call(f32[3072,256]{1,0:T(8,128)S(1)} %get-tuple-element.15.moved, bf16[2,2,16,16,256]{4,3,2,1,0:T(8,128)(2,1)S(1)} %get-tuple-element.16.full, ...), custom_call_target="tpu_custom_call" | custom-call | tf_op jit(solution)/shard_map/pallas_call | solution.py:713

commit v6 on v3

--- a/solution.py
+++ b/solution.py
@@ -465,8 +465,6 @@
         part_of = pl.ds(256 * half, 256)
         mixer_early[part_of, :] = product(act_t, part_of, early, second)
 
-    send_all("by", lambda peer: slot_part, slot_got.at[by], slot_sems.at[0], slot_sems.at[1])
-    slot_got[by] = slot_part[...]
     send_mate(head_grad, head_pair, (head_send.at[0], head_recv.at[0]))
 
     def head_line(axis, value):
@@ -543,6 +541,8 @@
     start_line(0)
     start_line(1)
     head_line(2, head_line_sum(1))
+    send_all("by", lambda peer: slot_part, slot_got.at[by], slot_sems.at[0], slot_sems.at[1])
+    slot_got[by] = slot_part[...]
     diffuse(0, field, y_edge, moved)
     start_plane_all(0)
     start_plane_all(1)

time: 41.6 us -> 42.4 us (1.019)
  Pallas kernels: 40.6 us -> 41.6 us
    pallas_call x1, Pallas kernels: 38.3 us -> 39.3 us  [per_device(): pl.pallas_call(step_kernel, out_shape=(pltpu.VMEM((COLS, CZ), F32), pltpu...]
where the time goes in v6:
time: 42.4 us; the launch traced here: 42.2 us
  Pallas kernels  41.6 us (98%)
  between operations  0.64 us (2%)
    pallas_call x1, Pallas kernels, per_device(): pl.pallas_call(step_kernel, out_shape=(pltpu.VMEM((COLS, CZ), F32), pltpu...  39.3 us
    pallas_call x1, Pallas kernels, per_device(): pl.pallas_call(finish_kernel, out_shape=(jax.ShapeDtypeStruct((COLS, CZ),...  2.31 us

profile of v6, /device:TPU:1, one launch (start us, length us, event | category | flops | bytes accessed | tf_op | source)
XLA Modules:
  0.0 42.2 jit_solution(12336821616687750997)
XLA Ops:
  0.6 39.3 %shard_map.110 = (f32[3072,256]{1,0:T(8,128)S(1)}, bf16[2,2,16,16,256]{4,3,2,1,0:T(8,128)(2,1)S(1)}, bf16[32,16,256]{2,1,0:T(8,128)(2,1)S(1)}, f32[8,256]{1,0:T(8,128)S(1)}, f32[8,128]{1,0:T(8,128)S(1)}) custom-call(s32[3,1,32]{2,1,0:T(1,128)} %corners_in.1, f32[128,24,256]{2,1,0:T(8,128)} %bitcast.4, s32[1,32]{1,0:T(1,128)} %bitcast.6, ...), custom_call_target="tpu_custom_call" | custom-call | tf_op jit(solution)/shard_map/pallas_call | solution.py:683
  39.9 2.3 %shard_map.111 = (f32[3072,256]{1,0:T(8,128)}, f32[3,1,64]{2,1,0:T(1,128)}, f32[256,512]{1,0:T(8,128)}, f32[512,512]{1,0:T(8,128)}, f32[3,512]{1,0:T(4,128)}) custom-call(f32[3072,256]{1,0:T(8,128)S(1)} %get-tuple-element.15.moved, bf16[2,2,16,16,256]{4,3,2,1,0:T(8,128)(2,1)S(1)} %get-tuple-element.16.full, ...), custom_call_target="tpu_custom_call" | custom-call | tf_op jit(solution)/shard_map/pallas_call | solution.py:707
